TPU v7x, 32 devices: a whole 2x2x4 slice. The times are simulated.
32 devices in a mesh: leaf: 32 (over z, y, x, core).
Axes of the slice: x: 2, y: 2, z: 4, core: 2. Of those that a mesh axis runs over, the one named last changes fastest.
Arguments:
- points: bfloat16 [32768, 512], P('leaf'), may hold values from -6 to 6
- weights: float32 [32768, 64], P('leaf'), may hold values from -6 to 6
- leaf_basis: float32 [32768, 256], P('leaf'), may hold values from -0.1875 to 0.1875
- transfer: float32 [32, 4, 256, 256], P('leaf'), may hold values from -0.375 to 0.375
- skeleton_index: int32 [5, 32, 256], replicated, may hold values from 0 to 1023, as said below
- node_owner: int32 [3, 32], replicated, may hold values from 0 to 7, as said below
- near_list: int32 [32, 3], replicated, may hold values from 0 to 7, as said below
Outputs:
- product: float32 [32768, 64], P('leaf')
Inputs may be any that keep to these rules, and one draw needn't show every extreme that they name: `near_list`: entry m > 0 of row i names leaf i XOR m of the same aligned group of 8 leaves; 0 marks an empty slot. The nonzero entries of a row are distinct and number 1 to 3; some row has 3. `skeleton_index`: row 0, column i: 256 distinct row numbers below 1024 within leaf i. Row m >= 1, column s below 32 >> m: 256 distinct row numbers below 512; other columns are unused. `node_owner`: row m - 1, column s below 32 >> m: a number below 2 to the power m; other columns are unused.
All inputs are finite; a program needn't handle non-finite values.
Results may differ from a plain program's by a relative error of at most 0.0018.
Values may be sent and summed in bfloat16 or wider, within the bound.
A program may use at most 128 MiB of HBM per device.

v0:
```python
import jax
import jax.numpy as jnp
from jax import lax
from jax.sharding import PartitionSpec as P

GROUP = 8


PRECISE = lax.Precision.HIGHEST


def swapped(value, axis, bit):
    mask = 2**bit
    pairs = [(source, source ^ mask) for source in range(lax.axis_size(axis))]
    return lax.ppermute(value, axis, pairs)


def for_sending(value):
    return jax.tree.map(lambda a: a.astype(jnp.bfloat16) if a.dtype == jnp.float32 else a, value)


def kernel_block(left_rows, right_rows):
    scale_factor = 2.0 / left_rows.shape[1]
    left_norm = jnp.sum(jnp.square(left_rows.astype(jnp.float32)), axis=1)
    right_norm = jnp.sum(jnp.square(right_rows.astype(jnp.float32)), axis=1)
    inner_products = lax.dot_general(
        left_rows, right_rows, (((1,), (1,)), ((), ())), preferred_element_type=jnp.float32
    )
    return jnp.exp(
        -scale_factor * (left_norm[:, None] + right_norm[None, :] - 2.0 * inner_products)
    )


def apply_matrix(matrix, values):
    return jnp.dot(matrix, values, precision=PRECISE, preferred_element_type=jnp.float32)


def apply_transposed(matrix, values):
    return lax.dot_general(
        matrix,
        values,
        (((0,), (0,)), ((), ())),
        precision=PRECISE,
        preferred_element_type=jnp.float32,
    )


def join_pair(held_part, arrived_part, upper_half):
    return jnp.where(
        upper_half,
        jnp.concatenate([arrived_part, held_part], 0),
        jnp.concatenate([held_part, arrived_part], 0),
    )


def group_collect(members, leaf_index, fetcher):
    stacked = tuple((member[None] for member in members))
    for bit_number in range(GROUP.bit_length() - 1):
        arrived = fetcher(stacked, bit_number)
        upper_half = leaf_index >> bit_number & 1 == 1
        stacked = tuple(
            (
                join_pair(held_part, arrived_part, upper_half)
                for held_part, arrived_part in zip(stacked, arrived)
            )
        )
    return stacked


def per_device(points, weights, leaf_basis, transfer, skeleton_index, node_owner, near_list):
    levels_count = lax.axis_size("leaf").bit_length() - 1
    leaf_index = lax.axis_index("leaf")
    position = leaf_index % GROUP
    group_start = leaf_index - position
    near_row = near_list[leaf_index]
    near_sum = apply_matrix(kernel_block(points, points), weights)

    def fetch_points(stacked, bit_number):
        return (swapped(stacked[0], "leaf", bit_number),)

    (group_points,) = group_collect((points,), leaf_index, fetch_points)

    def pushed_term(target_points):
        return apply_matrix(kernel_block(target_points, points), weights)

    def no_term(target_points):
        return jnp.zeros_like(near_sum)

    term_list = []
    for target in range(GROUP):
        wanted = jnp.any(near_list[group_start + target] == jnp.bitwise_xor(position, target)) & (
            position != target
        )
        pushed = lax.cond(wanted, pushed_term, no_term, group_points[target])
        term_list.append(jnp.where(position == target, near_sum, pushed))
    results = jnp.stack(term_list)
    for bit_number in reversed(range(GROUP.bit_length() - 1)):
        half_count = results.shape[0] // 2
        upper_half = leaf_index >> bit_number & 1 == 1
        kept_half = jnp.where(upper_half, results[half_count:], results[:half_count])
        sent_half = jnp.where(upper_half, results[:half_count], results[half_count:])
        results = kept_half + swapped(sent_half, "leaf", bit_number)
    near_sum = results[0]
    leaf_coeff = apply_transposed(leaf_basis, weights)
    leaf_rows = jnp.take(points, skeleton_index[0, leaf_index], axis=0)

    def fetch_skeletons(stacked, bit_number):
        return (
            swapped(for_sending(stacked[0]), "leaf", bit_number),
            swapped(stacked[1], "leaf", bit_number),
        )

    group_coeff, group_rows = group_collect((leaf_coeff, leaf_rows), leaf_index, fetch_skeletons)
    transfer_stack = transfer[0]

    def owns_node(height):
        if height == 0:
            return leaf_index >= 0
        return leaf_index % (1 << height) == node_owner[height - 1, leaf_index >> height]

    node_coeff = leaf_coeff
    node_rows = leaf_rows
    couplings = {}
    for height in range(levels_count):
        upper_half = leaf_index >> height & 1 == 1
        if height >= 3:
            sibling_rows = swapped(node_rows, "leaf", height)
            sibling_coeff = swapped(node_coeff, "leaf", height)
            couplings[height] = apply_matrix(kernel_block(node_rows, sibling_rows), sibling_coeff)
        else:
            sibling_rows = swapped(node_rows, "leaf", height)
        if height + 1 < levels_count:
            partial_value = jnp.where(
                owns_node(height), apply_transposed(transfer_stack[height], node_coeff), 0.0
            )
            for bit_number in range(height + 1):
                partial_value = partial_value + swapped(partial_value, "leaf", bit_number)
            node_coeff = partial_value
            joined = join_pair(node_rows, sibling_rows, upper_half)
            node_rows = jnp.take(
                joined, skeleton_index[height + 1, leaf_index >> height + 1], axis=0
            )
    down_field = couplings[levels_count - 1]
    for height in range(levels_count - 2, -1, -1):
        partial_value = jnp.where(
            owns_node(height), apply_matrix(transfer_stack[height], down_field), 0.0
        )
        for bit_number in range(height):
            partial_value = partial_value + swapped(partial_value, "leaf", bit_number)
        down_field = partial_value
        if height >= 3:
            down_field = down_field + couplings[height]

    def far_term(operands):
        return apply_matrix(kernel_block(leaf_rows, operands[0]), operands[1])

    def no_far(operands):
        return jnp.zeros_like(down_field)

    for target in range(GROUP):
        distant = (position != target) & jnp.logical_not(
            jnp.any(near_row == jnp.bitwise_xor(position, target))
        )
        down_field = down_field + lax.cond(
            distant, far_term, no_far, (group_rows[target], group_coeff[target])
        )
    return near_sum + apply_matrix(leaf_basis, down_field)


def solution(mesh):
    return jax.shard_map(
        per_device,
        mesh=mesh,
        in_specs=(
            P("leaf", None),
            P("leaf", None),
            P("leaf", None),
            P("leaf", None, None, None),
            P(),
            P(),
            P(),
        ),
        out_specs=P("leaf", None),
        check_vma=False,
    )
```

profile of v0, /device:TPU:0, one launch (start us, length us, event | category | flops | bytes accessed | tf_op | source)
XLA Modules:
  0.0 358.6 jit_solution(5689306491747704355)
XLA Ops:
  1.5 3.3 gather_fusion
  5.9 1.7 fusion.256
  8.4 1.8 bitcast_select_fusion
  11.3 3.2 maximum_select_fusion.2
  14.5 2.5 collective-permute-start.1
  21.9 5.8 %fusion.168 = f32[1024,64]{0,1:T(8,128)} fusion(f32[1024,64]{0,1:T(8,128)S(1)} %copy-done.21, f32[1024,1024]{1,0:T(8,128)S(1)} %fusion.255, f32[1024]{0:T(1024)S(1)} %multiply_reduce_fusion.32), kind=kOutput, calls=%fused_computation.223 | convolution fusion | flops 809500672 | bytes 4722688 | tf_op jit(solution)/shard_map/dot_general | solution.py:35
  27.6 35.9 %collective-permute-done.1 = bf16[2,1024,512]{2,1,0:T(8,128)(2,1)} collective-permute-done((bf16[2,1024,512]{2,1,0:T(8,128)(2,1)}, bf16[2,1024,512]{2,1,0:T(8,128)(2,1)}, u32[]{:S(2)}, u32[]{:S(2)}) %collective-permute-start.1) | collective-permute-done | bytes 2097184 | tf_op jit(solution)/shard_map/ppermute | solution.py:15
  63.6 5.2 %maximum_select_fusion.1 = bf16[4,1024,512]{2,1,0:T(8,128)(2,1)} fusion(bf16[2,1024,512]{2,1,0:T(8,128)(2,1)} %maximum_select_fusion.2, bf16[2,1024,512]{2,1,0:T(8,128)(2,1)} %collective-permute-done.1, pred[]{:T(512)S(6)} %eq.162), kind=kLoop, calls=%fused_computation.222 | loop fusion | flops 6291456 | bytes 8388609 | tf_op jit(solution)/shard_map/jit(_where)/select_n | solution.py:49
  68.8 1.8 collective-permute-start.2
  71.7 1.5 constant_dynamic-slice_fusion.15
  76.2 1.6 collective-permute-start.13
  82.7 1.9 fusion.186
  84.5 4.4 %collective-permute-done.7 = bf16[256,512]{1,0:T(8,128)(2,1)S(1)} collective-permute-done((bf16[256,512]{1,0:T(8,128)(2,1)S(1)}, bf16[256,512]{1,0:T(8,128)(2,1)S(1)}, u32[]{:S(2)}, u32[]{:S(2)}) %collective-permute-start.7) | collective-permute-done | bytes 262176 | tf_op jit(solution)/shard_map/ppermute | solution.py:15
  93.9 3.3 collective-permute-done.15
  97.3 1.6 collective-permute-start.16
  102.6 65.9 %collective-permute-done.16 = f32[256,64]{0,1:T(8,128)S(1)} collective-permute-done((f32[256,64]{0,1:T(8,128)S(1)}, f32[256,64]{0,1:T(8,128)S(1)}, u32[]{:S(2)}, u32[]{:S(2)}) %collective-permute-start.16) | collective-permute-done | bytes 65568 | tf_op jit(solution)/shard_map/ppermute | solution.py:15
  171.3 1.7 collective-permute-start.9
  174.3 2.2 maximum_select_fusion.9
  176.5 1.5 collective-permute-start.30
  179.3 1.5 collective-permute-start.33
  180.8 12.0 %collective-permute-done.18 = f32[256,64]{0,1:T(8,128)S(1)} collective-permute-done((f32[256,64]{0,1:T(8,128)S(1)}, f32[256,64]{0,1:T(8,128)S(1)}, u32[]{:S(2)}, u32[]{:S(2)}) %collective-permute-start.18) | collective-permute-done | bytes 65568 | tf_op jit(solution)/shard_map/ppermute | solution.py:15
  193.5 1.5 collective-permute-start.19
  195.2 1.9 gather_fusion.4
  198.2 2.7 collective-permute-start.10
  208.4 5.0 %collective-permute-done.20 = f32[256,64]{0,1:T(8,128)S(1)} collective-permute-done((f32[256,64]{0,1:T(8,128)S(1)}, f32[256,64]{0,1:T(8,128)S(1)}, u32[]{:S(2)}, u32[]{:S(2)}) %collective-permute-start.20) | collective-permute-done | bytes 65568 | tf_op jit(solution)/shard_map/ppermute | solution.py:15
  213.4 3.1 collective-permute-start.21
  216.5 2.7 maximum_select_fusion.4
  223.2 9.1 %maximum_select_fusion = bf16[8,1024,512]{2,1,0:T(8,128)(2,1)} fusion(bf16[4,1024,512]{2,1,0:T(8,128)(2,1)} %maximum_select_fusion.1, bf16[4,1024,512]{2,1,0:T(8,128)(2,1)} %collective-permute-done.2, pred[]{:T(512)S(6)} %eq.163), kind=kLoop, calls=%fused_computation.221 | loop fusion | flops 12582912 | bytes 16777216 | tf_op jit(solution)/shard_map/jit(_where)/select_n | solution.py:49
  233.2 10.3 %conditional.17 = (f32[1024,64]{0,1:T(8,128)S(1)}) conditional(s32[]{:T(128)} %convert_element_type.186, () %tuple.104, (bf16[8,1024,512]{2,1,0:T(8,128)(2,1)}, bf16[1024,512]{1,0:T(8,128)(2,1)S(1)}, f32[1024,64]{0,1:T(8,128)S(1)}) %tuple.241), branch_computations={%region_7.8_spmd, %region_8.11_spmd} | conditional | flops 1886386176 | bytes 14172196 | solution.py:94
  233.2 1.8 multiply_reduce_fusion.2
  235.1 2.5 fusion.25
  237.6 6.0 %fusion.15 = f32[1024,64]{0,1:T(8,128)S(1)} fusion(f32[1024,64]{0,1:T(8,128)} %copy-done.23, f32[1024,1024]{1,0:T(8,128)S(1)} %fusion.25, f32[1024]{0:T(1024)S(1)} %get-tuple-element.370, f32[1024]{0:T(1024)S(1)} %get-tuple-element.371), kind=kOutput, calls=%fused_computation.22 | convolution fusion | flops 809500672 | bytes 4726784 | tf_op jit(solution)/shard_map/cond/branch_1_fun/dot_general | solution.py:35
  246.9 6.3 %conditional.21 = (f32[1024,64]{0,1:T(8,128)S(1)}) conditional(s32[]{:T(128)} %convert_element_type.190, () %tuple.108, (bf16[8,1024,512]{2,1,0:T(8,128)(2,1)}, bf16[1024,512]{1,0:T(8,128)(2,1)S(1)}, f32[1024,64]{0,1:T(8,128)}) %tuple.237), branch_computations={%region_27.28_spmd, %region_28.31_spmd} | conditional | flops 1886386176 | bytes 14172196 | solution.py:94
  254.7 7.0 %conditional.23 = (f32[1024,64]{0,1:T(8,128)S(1)}) conditional(s32[]{:T(128)} %convert_element_type.192, () %tuple.110, (bf16[8,1024,512]{2,1,0:T(8,128)(2,1)}, bf16[1024,512]{1,0:T(8,128)(2,1)S(1)}, f32[1024,64]{0,1:T(8,128)}) %tuple.239), branch_computations={%region_37.38_spmd, %region_38.41_spmd} | conditional | flops 1886386176 | bytes 14172196 | solution.py:94
  262.5 1.8 select_bitcast_fusion.7
  264.3 1.4 fusion.194
  266.1 24.6 %collective-permute-start.22 = (f32[256,64]{0,1:T(8,128)S(1)}, f32[256,64]{0,1:T(8,128)S(1)}, u32[]{:S(2)}, u32[]{:S(2)}) collective-permute-start(f32[256,64]{0,1:T(8,128)S(1)} %fusion.184), channel_id=1, source_target_pairs={{0,1},{1,0},{2,3},{3,2},{4,5},{5,4},{6,7},{7,6},{8,9},{9,8},{10,11... | collective-permute-start | bytes 196616 | tf_op jit(solution)/shard_map/ppermute | solution.py:15
  291.8 4.2 %collective-permute-done.23 = f32[256,64]{0,1:T(8,128)S(1)} collective-permute-done((f32[256,64]{0,1:T(8,128)S(1)}, f32[256,64]{0,1:T(8,128)S(1)}, u32[]{:S(2)}, u32[]{:S(2)}) %collective-permute-start.23) | collective-permute-done | bytes 65568 | tf_op jit(solution)/shard_map/ppermute | solution.py:15
  296.1 1.8 collective-permute-start.24
  297.9 1.3 fusion.203
  299.2 2.0 collective-permute-done.24
  301.5 4.4 %collective-permute-start.26 = (f32[256,64]{0,1:T(8,128)S(1)}, f32[256,64]{0,1:T(8,128)S(1)}, u32[]{:S(2)}, u32[]{:S(2)}) collective-permute-start(f32[256,64]{0,1:T(8,128)S(1)} %fusion.183), channel_id=1, source_target_pairs={{0,1},{1,0},{2,3},{3,2},{4,5},{5,4},{6,7},{7,6},{8,9},{9,8},{10,11... | collective-permute-start | bytes 196616 | tf_op jit(solution)/shard_map/ppermute | solution.py:15
  312.0 2.0 select_add_fusion
  314.9 2.0 collective-permute-start.4
  316.9 2.0 fusion.182
  318.9 3.9 %maximum_select_fusion.3 = bf16[8,256,512]{2,1,0:T(8,128)(2,1)} fusion(bf16[4,256,512]{2,1,0:T(8,128)(2,1)} %maximum_select_fusion.4, bf16[4,256,512]{2,1,0:T(8,128)(2,1)} %collective-permute-done.31, pred[]{:T(512)S(6)} %eq.163), kind=kLoop, calls=%fused_computation.230 | loop fusion | flops 3145728 | bytes 4194305 | tf_op jit(solution)/shard_map/jit(_where)/select_n | solution.py:49
  322.9 5.0 %conditional.25 = (f32[256,64]{0,1:T(8,128)S(1)}) conditional(s32[]{:T(128)} %convert_element_type.205, () %tuple.113, (bf16[256,512]{1,0:T(8,128)(2,1)S(1)}, bf16[8,256,512]{2,1,0:T(8,128)(2,1)}, f32[8,256,64]{1,2,0:T(8,128)S(1)}) %tuple.128), branch_computations={%region_51.53_spmd, %region_52.56_spmd} | conditional | flops 118488576 | bytes 2822152 | solution.py:164
  325.2 1.3 copy.33
  326.6 1.3 fusion.131
  327.9 5.0 %conditional.27 = (f32[256,64]{0,1:T(8,128)S(1)}) conditional(s32[]{:T(128)} %convert_element_type.207, () %tuple.115, (bf16[256,512]{1,0:T(8,128)(2,1)S(1)}, bf16[8,256,512]{2,1,0:T(8,128)(2,1)}, f32[8,256,64]{1,2,0:T(8,128)S(1)}) %tuple.128), branch_computations={%region_61.63_spmd, %region_62.66_spmd} | conditional | flops 118488576 | bytes 2822152 | solution.py:164
  330.3 1.3 copy.35
  332.9 5.2 %conditional.28 = (f32[256,64]{0,1:T(8,128)S(1)}) conditional(s32[]{:T(128)} %convert_element_type.208, () %tuple.116, (bf16[256,512]{1,0:T(8,128)(2,1)S(1)}, bf16[8,256,512]{2,1,0:T(8,128)(2,1)}, f32[8,256,64]{1,2,0:T(8,128)S(1)}) %tuple.128), branch_computations={%region_66.68_spmd, %region_67.71_spmd} | conditional | flops 118488576 | bytes 2822152 | solution.py:164
  335.5 1.3 copy.36
  336.9 1.3 fusion.149
  338.1 5.0 %conditional.29 = (f32[256,64]{0,1:T(8,128)S(1)}) conditional(s32[]{:T(128)} %convert_element_type.209, () %tuple.117, (bf16[256,512]{1,0:T(8,128)(2,1)S(1)}, bf16[8,256,512]{2,1,0:T(8,128)(2,1)}, f32[8,256,64]{1,2,0:T(8,128)S(1)}) %tuple.128), branch_computations={%region_71.73_spmd, %region_72.76_spmd} | conditional | flops 118488576 | bytes 2822152 | solution.py:164
  340.5 1.3 copy.37
  341.8 1.3 fusion.155
  343.1 5.6 %conditional.30 = (f32[256,64]{0,1:T(8,128)}) conditional(s32[]{:T(128)} %convert_element_type.210, () %tuple.118, (bf16[256,512]{1,0:T(8,128)(2,1)S(1)}, bf16[8,256,512]{2,1,0:T(8,128)(2,1)}, f32[8,256,64]{1,2,0:T(8,128)S(1)}) %tuple.128), branch_computations={%region_76.78_spmd, %region_77.81_spmd} | conditional | flops 118488576 | bytes 2822152 | solution.py:164
  345.5 1.3 copy.38
  346.8 1.9 fusion.161
  348.8 5.0 %conditional.31 = (f32[256,64]{0,1:T(8,128)S(1)}) conditional(s32[]{:T(128)} %convert_element_type.211, () %tuple.119, (bf16[256,512]{1,0:T(8,128)(2,1)S(1)}, bf16[8,256,512]{2,1,0:T(8,128)(2,1)}, f32[8,256,64]{1,2,0:T(8,128)S(1)}) %tuple.128), branch_computations={%region_81.83_spmd, %region_82.86_spmd} | conditional | flops 118488576 | bytes 2822152 | solution.py:164
  351.1 1.3 copy.39
  352.4 1.3 fusion.167
  355.0 1.4 fusion.193
  (199 shorter events, 67.8 us)
Async XLA Ops:
  0.0 5.9 %copy-start = (f32[1024,256]{1,0:T(8,128)S(1)}, f32[1024,256]{1,0:T(8,128)}, u32[]{:S(2)}) copy-start(f32[1024,256]{1,0:T(8,128)} %param.43) | copy-start | bytes 3145732
  0.0 11.3 %copy-start.1 = (bf16[1024,512]{1,0:T(8,128)(2,1)S(1)}, bf16[1024,512]{1,0:T(8,128)(2,1)}, u32[]{:S(2)}) copy-start(bf16[1024,512]{1,0:T(8,128)(2,1)} %param.41) | copy-start | bytes 3145732
  0.0 7.6 %copy-start.2 = (f32[1,4,256,256]{3,2,1,0:T(8,128)S(1)}, f32[1,4,256,256]{3,2,1,0:T(8,128)}, u32[]{:S(2)}) copy-start(f32[1,4,256,256]{3,2,1,0:T(8,128)} %param.44) | copy-start | bytes 3145732
  0.0 11.3 %collective-permute-start = (bf16[1,1024,512]{2,1,0:T(8,128)(2,1)}, bf16[1,1024,512]{2,1,0:T(8,128)(2,1)}, u32[]{:S(2)}, u32[]{:S(2)}) collective-permute-start(bf16[1,1024,512]{2,1,0:T(8,128)(2,1)} %bitcast.225), channel_id=1, source_target_pairs={{0,1},{1,0},{2,3},{3,2},{4,5},{5,4},{6,7},{7,6},{8,9},{9,8},{10,11... | collective-permute-start | bytes 3145736 | tf_op jit(solution)/shard_map/ppermute | solution.py:15
  5.8 71.9 %collective-permute-start.6 = (bf16[256,512]{1,0:T(8,128)(2,1)S(1)}, bf16[256,512]{1,0:T(8,128)(2,1)}, u32[]{:S(2)}, u32[]{:S(2)}) collective-permute-start(bf16[256,512]{1,0:T(8,128)(2,1)S(1)} %broadcast_select_fusion.4), channel_id=1, source_target_pairs={{0,1},{1,0},{2,3},{3,2},{4,5},{5,4},{6,7},{7,6},{8,9},{9,8},{10,11... | collective-permute-start | bytes 786440 | tf_op jit(solution)/shard_map/ppermute | solution.py:15
  7.9 65.8 %collective-permute-start.11 = (f32[256,64]{0,1:T(8,128)S(1)}, f32[256,64]{0,1:T(8,128)}, u32[]{:S(2)}, u32[]{:S(2)}) collective-permute-start(f32[256,64]{0,1:T(8,128)S(1)} %fusion.188), channel_id=1, source_target_pairs={{0,1},{1,0},{2,3},{3,2},{4,5},{5,4},{6,7},{7,6},{8,9},{9,8},{10,11... | collective-permute-start | bytes 196616 | tf_op jit(solution)/shard_map/ppermute | solution.py:15
  10.2 164.2 %collective-permute-start.29 = (bf16[1,256,512]{2,1,0:T(8,128)(2,1)}, bf16[1,256,512]{2,1,0:T(8,128)(2,1)}, u32[]{:S(2)}, u32[]{:S(2)}) collective-permute-start(bf16[1,256,512]{2,1,0:T(8,128)(2,1)} %bitcast_select_fusion), channel_id=1, source_target_pairs={{0,1},{1,0},{2,3},{3,2},{4,5},{5,4},{6,7},{7,6},{8,9},{9,8},{10,11... | collective-permute-start | bytes 786440 | tf_op jit(solution)/shard_map/ppermute | solution.py:15
  10.8 91.0 %collective-permute-start.32 = (bf16[1,256,64]{1,2,0:T(8,128)(2,1)}, bf16[1,256,64]{1,2,0:T(8,128)(2,1)}, u32[]{:S(2)}, u32[]{:S(2)}) collective-permute-start(bf16[1,256,64]{1,2,0:T(8,128)(2,1)} %convert_bitcast_fusion), channel_id=1, source_target_pairs={{0,1},{1,0},{2,3},{3,2},{4,5},{5,4},{6,7},{7,6},{8,9},{9,8},{10,11... | collective-permute-start | bytes 98312 | tf_op jit(solution)/shard_map/ppermute | solution.py:15
  14.5 49.0 %collective-permute-start.1 = (bf16[2,1024,512]{2,1,0:T(8,128)(2,1)}, bf16[2,1024,512]{2,1,0:T(8,128)(2,1)}, u32[]{:S(2)}, u32[]{:S(2)}) collective-permute-start(bf16[2,1024,512]{2,1,0:T(8,128)(2,1)} %maximum_select_fusion.2), channel_id=1, source_target_pairs={{0,2},{1,3},{2,0},{3,1},{4,6},{5,7},{6,4},{7,5},{8,10},{9,11},{10,... | collective-permute-start | bytes 6291464 | tf_op jit(solution)/shard_map/ppermute | solution.py:15
  17.7 0.6 copy-start.33
  17.7 2.8 copy-start.31
  20.6 1.3 copy-start.21
  27.6 42.9 %copy-start.32 = (s32[1,1,256]{2,1,0:T(1,128)S(1)}, s32[1,1,256]{2,1,0:T(1,128)}, u32[]{:S(2)}) copy-start(s32[1,1,256]{2,1,0:T(1,128)} %copy-done.31) | copy-start | bytes 3076
  68.8 154.3 %collective-permute-start.2 = (bf16[4,1024,512]{2,1,0:T(8,128)(2,1)}, bf16[4,1024,512]{2,1,0:T(8,128)(2,1)}, u32[]{:S(2)}, u32[]{:S(2)}) collective-permute-start(bf16[4,1024,512]{2,1,0:T(8,128)(2,1)} %maximum_select_fusion.1), channel_id=1, source_target_pairs={{0,4},{1,5},{2,6},{3,7},{4,0},{5,1},{6,2},{7,3},{8,12},{9,13},{10,... | collective-permute-start | bytes 12582920 | tf_op jit(solution)/shard_map/ppermute | solution.py:15
  74.8 1.3 collective-permute-start.12
  76.2 22.7 %copy-start.30 = (s32[32,3]{0,1:T(4,128)S(1)}, s32[32,3]{0,1:T(4,128)}, u32[]{:S(2)}) copy-start(s32[32,3]{0,1:T(4,128)} %param.47) | copy-start | bytes 1156
  76.2 6.5 %collective-permute-start.13 = (f32[256,64]{0,1:T(8,128)S(1)}, f32[256,64]{0,1:T(8,128)}, u32[]{:S(2)}, u32[]{:S(2)}) collective-permute-start(f32[256,64]{0,1:T(8,128)S(1)} %add.493), channel_id=1, source_target_pairs={{0,2},{1,3},{2,0},{3,1},{4,6},{5,7},{6,4},{7,5},{8,10},{9,11},{10,... | collective-permute-start | bytes 196616 | tf_op jit(solution)/shard_map/ppermute | solution.py:15
  80.7 8.2 %collective-permute-start.7 = (bf16[256,512]{1,0:T(8,128)(2,1)S(1)}, bf16[256,512]{1,0:T(8,128)(2,1)S(1)}, u32[]{:S(2)}, u32[]{:S(2)}) collective-permute-start(bf16[256,512]{1,0:T(8,128)(2,1)S(1)} %broadcast_select_fusion.3), channel_id=1, source_target_pairs={{0,2},{1,3},{2,0},{3,1},{4,6},{5,7},{6,4},{7,5},{8,10},{9,11},{10,... | collective-permute-start | bytes 786440 | tf_op jit(solution)/shard_map/ppermute | solution.py:15
  84.5 7.5 %collective-permute-start.14 = (f32[256,64]{0,1:T(8,128)}, f32[256,64]{0,1:T(8,128)S(1)}, u32[]{:S(2)}, u32[]{:S(2)}) collective-permute-start(f32[256,64]{0,1:T(8,128)} %fusion.186), channel_id=1, source_target_pairs={{0,1},{1,0},{2,3},{3,2},{4,5},{5,4},{6,7},{7,6},{8,9},{9,8},{10,11... | collective-permute-start | bytes 196616 | tf_op jit(solution)/shard_map/ppermute | solution.py:15
  91.0 78.1 %collective-permute-start.8 = (bf16[256,512]{1,0:T(8,128)(2,1)S(1)}, bf16[256,512]{1,0:T(8,128)(2,1)S(1)}, u32[]{:S(2)}, u32[]{:S(2)}) collective-permute-start(bf16[256,512]{1,0:T(8,128)(2,1)S(1)} %broadcast_select_fusion.2), channel_id=1, source_target_pairs={{0,4},{1,5},{2,6},{3,7},{4,0},{5,1},{6,2},{7,3},{8,12},{9,13},{10,... | collective-permute-start | bytes 786440 | tf_op jit(solution)/shard_map/ppermute | solution.py:15
  92.9 4.3 %collective-permute-start.15 = (f32[256,64]{0,1:T(8,128)S(1)}, f32[256,64]{0,1:T(8,128)S(1)}, u32[]{:S(2)}, u32[]{:S(2)}) collective-permute-start(f32[256,64]{0,1:T(8,128)S(1)} %add.495), channel_id=1, source_target_pairs={{0,2},{1,3},{2,0},{3,1},{4,6},{5,7},{6,4},{7,5},{8,10},{9,11},{10,... | collective-permute-start | bytes 196616 | tf_op jit(solution)/shard_map/ppermute | solution.py:15
  97.3 71.2 %collective-permute-start.16 = (f32[256,64]{0,1:T(8,128)S(1)}, f32[256,64]{0,1:T(8,128)S(1)}, u32[]{:S(2)}, u32[]{:S(2)}) collective-permute-start(f32[256,64]{0,1:T(8,128)S(1)} %add.496), channel_id=1, source_target_pairs={{0,4},{1,5},{2,6},{3,7},{4,0},{5,1},{6,2},{7,3},{8,12},{9,13},{10,... | collective-permute-start | bytes 196616 | tf_op jit(solution)/shard_map/ppermute | solution.py:15
  169.3 27.8 %copy-start.34 = (pred[256]{0:T(512)(128)(4,1)S(1)}, pred[256]{0:T(512)(128)(4,1)}, u32[]{:S(2)}) copy-start(pred[256]{0:T(512)(128)(4,1)} %compare_and_fusion) | copy-start | bytes 772
  171.3 23.7 %collective-permute-start.9 = (bf16[256,512]{1,0:T(8,128)(2,1)S(1)}, bf16[256,512]{1,0:T(8,128)(2,1)S(1)}, u32[]{:S(2)}, u32[]{:S(2)}) collective-permute-start(bf16[256,512]{1,0:T(8,128)(2,1)S(1)} %get-tuple-element.361), channel_id=1, source_target_pairs={{0,8},{1,9},{2,10},{3,11},{4,12},{5,13},{6,14},{7,15},{8,0},{9,1},... | collective-permute-start | bytes 786440 | tf_op jit(solution)/shard_map/ppermute | solution.py:15
  174.3 3.8 %collective-permute-start.17 = (f32[256,64]{0,1:T(8,128)S(1)}, f32[256,64]{0,1:T(8,128)S(1)}, u32[]{:S(2)}, u32[]{:S(2)}) collective-permute-start(f32[256,64]{0,1:T(8,128)S(1)} %fusion.185), channel_id=1, source_target_pairs={{0,1},{1,0},{2,3},{3,2},{4,5},{5,4},{6,7},{7,6},{8,9},{9,8},{10,11... | collective-permute-start | bytes 196616 | tf_op jit(solution)/shard_map/ppermute | solution.py:15
  176.5 36.9 %collective-permute-start.30 = (bf16[2,256,512]{2,1,0:T(8,128)(2,1)}, bf16[2,256,512]{2,1,0:T(8,128)(2,1)}, u32[]{:S(2)}, u32[]{:S(2)}) collective-permute-start(bf16[2,256,512]{2,1,0:T(8,128)(2,1)} %maximum_select_fusion.9), channel_id=1, source_target_pairs={{0,2},{1,3},{2,0},{3,1},{4,6},{5,7},{6,4},{7,5},{8,10},{9,11},{10,... | collective-permute-start | bytes 1572872 | tf_op jit(solution)/shard_map/ppermute | solution.py:15
  178.0 14.8 %collective-permute-start.18 = (f32[256,64]{0,1:T(8,128)S(1)}, f32[256,64]{0,1:T(8,128)S(1)}, u32[]{:S(2)}, u32[]{:S(2)}) collective-permute-start(f32[256,64]{0,1:T(8,128)S(1)} %add.498), channel_id=1, source_target_pairs={{0,2},{1,3},{2,0},{3,1},{4,6},{5,7},{6,4},{7,5},{8,10},{9,11},{10,... | collective-permute-start | bytes 196616 | tf_op jit(solution)/shard_map/ppermute | solution.py:15
  179.3 27.8 %copy-start.20 = (f32[2,256,64]{1,2,0:T(8,128)S(1)}, f32[2,256,64]{1,2,0:T(8,128)}, u32[]{:S(2)}) copy-start(f32[2,256,64]{1,2,0:T(8,128)} %get-tuple-element.365) | copy-start | bytes 393220
  179.3 25.5 %collective-permute-start.33 = (bf16[2,256,64]{1,2,0:T(8,128)(2,1)}, bf16[2,256,64]{1,2,0:T(8,128)(2,1)}, u32[]{:S(2)}, u32[]{:S(2)}) collective-permute-start(bf16[2,256,64]{1,2,0:T(8,128)(2,1)} %get-tuple-element.364), channel_id=1, source_target_pairs={{0,2},{1,3},{2,0},{3,1},{4,6},{5,7},{6,4},{7,5},{8,10},{9,11},{10,... | collective-permute-start | bytes 196616 | tf_op jit(solution)/shard_map/ppermute | solution.py:15
  193.5 12.2 %collective-permute-start.19 = (f32[256,64]{0,1:T(8,128)}, f32[256,64]{0,1:T(8,128)}, u32[]{:S(2)}, u32[]{:S(2)}) collective-permute-start(f32[256,64]{0,1:T(8,128)} %add.499), channel_id=1, source_target_pairs={{0,4},{1,5},{2,6},{3,7},{4,0},{5,1},{6,2},{7,3},{8,12},{9,13},{10,... | collective-permute-start | bytes 196616 | tf_op jit(solution)/shard_map/ppermute | solution.py:15
  198.2 20.9 %collective-permute-start.10 = (bf16[256,512]{1,0:T(8,128)(2,1)S(1)}, bf16[256,512]{1,0:T(8,128)(2,1)S(1)}, u32[]{:S(2)}, u32[]{:S(2)}) collective-permute-start(bf16[256,512]{1,0:T(8,128)(2,1)S(1)} %get-tuple-element.359), channel_id=1, source_target_pairs={{0,16},{1,17},{2,18},{3,19},{4,20},{5,21},{6,22},{7,23},{8,24},{9,... | collective-permute-start | bytes 786440 | tf_op jit(solution)/shard_map/ppermute | solution.py:15
  206.6 6.8 %collective-permute-start.20 = (f32[256,64]{0,1:T(8,128)S(1)}, f32[256,64]{0,1:T(8,128)S(1)}, u32[]{:S(2)}, u32[]{:S(2)}) collective-permute-start(f32[256,64]{0,1:T(8,128)S(1)} %add.500), channel_id=1, source_target_pairs={{0,8},{1,9},{2,10},{3,11},{4,12},{5,13},{6,14},{7,15},{8,0},{9,1},... | collective-permute-start | bytes 196616 | tf_op jit(solution)/shard_map/ppermute | solution.py:15
  207.9 103.1 %collective-permute-start.34 = (bf16[4,256,64]{1,2,0:T(8,128)(2,1)}, bf16[4,256,64]{1,2,0:T(8,128)(2,1)}, u32[]{:S(2)}, u32[]{:S(2)}) collective-permute-start(bf16[4,256,64]{1,2,0:T(8,128)(2,1)} %get-tuple-element.362), channel_id=1, source_target_pairs={{0,4},{1,5},{2,6},{3,7},{4,0},{5,1},{6,2},{7,3},{8,12},{9,13},{10,... | collective-permute-start | bytes 393224 | tf_op jit(solution)/shard_map/ppermute | solution.py:15
  213.4 84.5 %collective-permute-start.25 = (f32[256,64]{0,1:T(8,128)}, f32[256,64]{0,1:T(8,128)}, u32[]{:S(2)}, u32[]{:S(2)}) collective-permute-start(f32[256,64]{0,1:T(8,128)} %add.497), channel_id=1, source_target_pairs={{0,8},{1,9},{2,10},{3,11},{4,12},{5,13},{6,14},{7,15},{8,0},{9,1},... | collective-permute-start | bytes 196616 | tf_op jit(solution)/shard_map/ppermute | solution.py:15
  213.4 9.3 %collective-permute-start.21 = (f32[256,64]{0,1:T(8,128)S(1)}, f32[256,64]{0,1:T(8,128)S(1)}, u32[]{:S(2)}, u32[]{:S(2)}) collective-permute-start(f32[256,64]{0,1:T(8,128)S(1)} %add.501), channel_id=1, source_target_pairs={{0,16},{1,17},{2,18},{3,19},{4,20},{5,21},{6,22},{7,23},{8,24},{9,... | collective-permute-start | bytes 196616 | tf_op jit(solution)/shard_map/ppermute | solution.py:15
  219.2 0.7 copy-start.10
  219.9 99.0 %collective-permute-start.31 = (bf16[4,256,512]{2,1,0:T(8,128)(2,1)}, bf16[4,256,512]{2,1,0:T(8,128)(2,1)}, u32[]{:S(2)}, u32[]{:S(2)}) collective-permute-start(bf16[4,256,512]{2,1,0:T(8,128)(2,1)} %maximum_select_fusion.4), channel_id=1, source_target_pairs={{0,4},{1,5},{2,6},{3,7},{4,0},{5,1},{6,2},{7,3},{8,12},{9,13},{10,... | collective-permute-start | bytes 3145736 | tf_op jit(solution)/shard_map/ppermute | solution.py:15
  223.1 9.2 %copy-start.22 = (f32[1024,64]{0,1:T(8,128)S(1)}, f32[1024,64]{0,1:T(8,128)}, u32[]{:S(2)}) copy-start(f32[1024,64]{0,1:T(8,128)} %param.42) | copy-start | bytes 786436
  232.5 0.7 copy-start.11
  233.2 4.3 %copy-start.23 = (f32[1024,64]{0,1:T(8,128)}, f32[1024,64]{0,1:T(8,128)S(1)}, u32[]{:S(2)}) copy-start(f32[1024,64]{0,1:T(8,128)S(1)} %get-tuple-element.299) | copy-start | bytes 786436 | tf_op jit(solution)/shard_map/cond
  243.6 0.7 copy-start.12
  244.3 0.7 copy-start.13
  245.5 0.7 copy-start.14
  246.2 0.7 copy-start.15
  253.3 0.7 copy-start.16
  254.0 0.7 copy-start.17
  261.8 0.7 copy-start.18
  262.5 3.2 copy-start.3
  264.3 37.2 %copy-start.4 = (f32[1,1024,64]{1,2,0:T(8,128)}, f32[1,1024,64]{1,2,0:T(8,128)S(1)}, u32[]{:S(2)}) copy-start(f32[1,1024,64]{1,2,0:T(8,128)S(1)} %get-tuple-element.402) | copy-start | bytes 786436
  264.3 41.7 %copy-start.5 = (f32[1,1024,64]{1,2,0:T(8,128)}, f32[1,1024,64]{1,2,0:T(8,128)S(1)}, u32[]{:S(2)}) copy-start(f32[1,1024,64]{1,2,0:T(8,128)S(1)} %get-tuple-element.403) | copy-start | bytes 786436
  264.3 41.7 %copy-start.6 = (f32[1,1024,64]{1,2,0:T(8,128)}, f32[1,1024,64]{1,2,0:T(8,128)S(1)}, u32[]{:S(2)}) copy-start(f32[1,1024,64]{1,2,0:T(8,128)S(1)} %get-tuple-element.404) | copy-start | bytes 786436
  264.3 41.7 %copy-start.7 = (f32[1,1024,64]{1,2,0:T(8,128)}, f32[1,1024,64]{1,2,0:T(8,128)S(1)}, u32[]{:S(2)}) copy-start(f32[1,1024,64]{1,2,0:T(8,128)S(1)} %get-tuple-element.405) | copy-start | bytes 786436
  264.3 41.7 %copy-start.8 = (f32[1,1024,64]{1,2,0:T(8,128)}, f32[1,1024,64]{1,2,0:T(8,128)S(1)}, u32[]{:S(2)}) copy-start(f32[1,1024,64]{1,2,0:T(8,128)S(1)} %get-tuple-element.406) | copy-start | bytes 786436
  264.3 41.7 %copy-start.9 = (f32[1,1024,64]{1,2,0:T(8,128)}, f32[1,1024,64]{1,2,0:T(8,128)S(1)}, u32[]{:S(2)}) copy-start(f32[1,1024,64]{1,2,0:T(8,128)S(1)} %get-tuple-element.407) | copy-start | bytes 786436
  265.7 46.3 %collective-permute-start.3 = (f32[4,1024,64]{1,2,0:T(8,128)}, f32[4,1024,64]{1,2,0:T(8,128)}, u32[]{:S(2)}, u32[]{:S(2)}) collective-permute-start(f32[4,1024,64]{1,2,0:T(8,128)} %fusion.194), channel_id=1, source_target_pairs={{0,4},{1,5},{2,6},{3,7},{4,0},{5,1},{6,2},{7,3},{8,12},{9,13},{10,... | collective-permute-start | bytes 3145736 | tf_op jit(solution)/shard_map/ppermute | solution.py:15
  266.1 25.5 %collective-permute-start.22 = (f32[256,64]{0,1:T(8,128)S(1)}, f32[256,64]{0,1:T(8,128)S(1)}, u32[]{:S(2)}, u32[]{:S(2)}) collective-permute-start(f32[256,64]{0,1:T(8,128)S(1)} %fusion.184), channel_id=1, source_target_pairs={{0,1},{1,0},{2,3},{3,2},{4,5},{5,4},{6,7},{7,6},{8,9},{9,8},{10,11... | collective-permute-start | bytes 196616 | tf_op jit(solution)/shard_map/ppermute | solution.py:15
  291.0 25.9 %copy-start.19 = (f32[4,256,64]{1,2,0:T(8,128)S(1)}, f32[4,256,64]{1,2,0:T(8,128)}, u32[]{:S(2)}) copy-start(f32[4,256,64]{1,2,0:T(8,128)} %get-tuple-element.363) | copy-start | bytes 786436
  291.6 4.4 %collective-permute-start.23 = (f32[256,64]{0,1:T(8,128)S(1)}, f32[256,64]{0,1:T(8,128)S(1)}, u32[]{:S(2)}, u32[]{:S(2)}) collective-permute-start(f32[256,64]{0,1:T(8,128)S(1)} %add.502), channel_id=1, source_target_pairs={{0,2},{1,3},{2,0},{3,1},{4,6},{5,7},{6,4},{7,5},{8,10},{9,11},{10,... | collective-permute-start | bytes 196616 | tf_op jit(solution)/shard_map/ppermute | solution.py:15
  296.1 5.1 %collective-permute-start.24 = (f32[256,64]{0,1:T(8,128)S(1)}, f32[256,64]{0,1:T(8,128)S(1)}, u32[]{:S(2)}, u32[]{:S(2)}) collective-permute-start(f32[256,64]{0,1:T(8,128)S(1)} %add.503), channel_id=1, source_target_pairs={{0,4},{1,5},{2,6},{3,7},{4,0},{5,1},{6,2},{7,3},{8,12},{9,13},{10,... | collective-permute-start | bytes 196616 | tf_op jit(solution)/shard_map/ppermute | solution.py:15
  301.5 10.4 %collective-permute-start.26 = (f32[256,64]{0,1:T(8,128)S(1)}, f32[256,64]{0,1:T(8,128)S(1)}, u32[]{:S(2)}, u32[]{:S(2)}) collective-permute-start(f32[256,64]{0,1:T(8,128)S(1)} %fusion.183), channel_id=1, source_target_pairs={{0,1},{1,0},{2,3},{3,2},{4,5},{5,4},{6,7},{7,6},{8,9},{9,8},{10,11... | collective-permute-start | bytes 196616 | tf_op jit(solution)/shard_map/ppermute | solution.py:15
  312.0 5.0 %collective-permute-start.27 = (f32[256,64]{0,1:T(8,128)S(1)}, f32[256,64]{0,1:T(8,128)S(1)}, u32[]{:S(2)}, u32[]{:S(2)}) collective-permute-start(f32[256,64]{0,1:T(8,128)S(1)} %add.509), channel_id=1, source_target_pairs={{0,2},{1,3},{2,0},{3,1},{4,6},{5,7},{6,4},{7,5},{8,10},{9,11},{10,... | collective-permute-start | bytes 196616 | tf_op jit(solution)/shard_map/ppermute | solution.py:15
  314.9 38.9 %collective-permute-start.4 = (f32[2,1024,64]{1,2,0:T(8,128)}, f32[2,1024,64]{1,2,0:T(8,128)}, u32[]{:S(2)}, u32[]{:S(2)}) collective-permute-start(f32[2,1024,64]{1,2,0:T(8,128)} %slice_select_fusion), channel_id=1, source_target_pairs={{0,2},{1,3},{2,0},{3,1},{4,6},{5,7},{6,4},{7,5},{8,10},{9,11},{10,... | collective-permute-start | bytes 1572872 | tf_op jit(solution)/shard_map/ppermute | solution.py:15
  318.9 36.1 %collective-permute-start.28 = (f32[256,64]{0,1:T(8,128)}, f32[256,64]{0,1:T(8,128)}, u32[]{:S(2)}, u32[]{:S(2)}) collective-permute-start(f32[256,64]{0,1:T(8,128)} %fusion.182), channel_id=1, source_target_pairs={{0,1},{1,0},{2,3},{3,2},{4,5},{5,4},{6,7},{7,6},{8,9},{9,8},{10,11... | collective-permute-start | bytes 196616 | tf_op jit(solution)/shard_map/ppermute | solution.py:15
  354.9 2.6 collective-permute-start.5
where the time goes:
time: 363 us; the launch traced here: 359 us
  waiting for transfers between devices  135 us (37%)
  other arithmetic  67.3 us (19%)
  starting transfers between devices  57.9 us (16%)
  matrix products  45.8 us (13%)
  local copies, waits for them, and re-layouts  25.6 us (7%)
  loops' own time  14.4 us (4%)
  between operations  13.1 us (4%)
    ppermute x35, waiting for transfers between devices, swapped(): return lax.ppermute(value, axis, pairs)  135 us
    ppermute x35, starting transfers between devices, swapped(): return lax.ppermute(value, axis, pairs)  57.9 us
    select_n x11, other arithmetic, join_pair(): jnp.where(upper_half, jnp.concatenate([arrived_part, held_part], 0), jnp....  28.2 us
    dot_general x15, matrix products, apply_matrix(): jnp.dot(matrix, values, precision=PRECISE, preferred_element_type=jnp.flo...  27.1 us
    another operation x8, loops' own time, per_device(): pushed = lax.cond(wanted, pushed_term, no_term, group_points[target])  14 us
    dot_general x10, matrix products, kernel_block(): lax.dot_general(left_rows, right_rows, (((1,), (1,)), ((), ())), preferre...  12.6 us
    reduce_sum x9, other arithmetic, kernel_block(): right_norm = jnp.sum(jnp.square(right_rows.astype(jnp.float32)), axis=1)  9.77 us
    another operation x15, local copies, waits for them, and re-layouts  8.09 us
  transfers between devices with their start and end apart: 35, of which 10 were waited for; matrix products, arithmetic and copies ran while one was open for 37% of the time, Pallas kernels for 0%

commit v1 on v0

v1 whole, which is shorter than its diff:
```python
import functools

import jax
import jax.numpy as jnp
from jax import lax
from jax.experimental import pallas as pl
from jax.experimental.pallas import tpu as pltpu
from jax.sharding import PartitionSpec as P

MESH = pl.DeviceIdType.MESH
GROUP = 8
CHUNKS = 4
TOP = 3
F32 = jnp.float32
BF16 = jnp.bfloat16
PRECISE = lax.Precision.HIGHEST


def split(value):
    high = value.astype(BF16)
    return high, (value - high.astype(F32)).astype(BF16)


def mm(left, right, precision=None):
    return jnp.dot(left, right, precision=precision, preferred_element_type=F32)


def mm_nt(left, right, precision=None):
    return lax.dot_general(
        left, right, (((1,), (1,)), ((), ())), precision=precision, preferred_element_type=F32
    )


def as_row(column):
    return jnp.broadcast_to(column, (column.shape[0], 128)).T[:1]


def as_column(row):
    return jnp.broadcast_to(row, (128, row.shape[1])).T[:, :1]


def norm_column(rows, scale):
    wide = rows.astype(F32)
    return -scale * jnp.sum(wide * wide, axis=1, keepdims=True)


def gauss(left, left_norm, right, right_norm, scale):
    return jnp.exp((2.0 * scale) * mm_nt(left, right) + (left_norm + right_norm))


def contract(coeff, block):
    high, low = split(block)
    return mm(coeff, high) + mm(coeff, low)


def contract_both(coeff_high, coeff_low, block):
    high, low = split(block)
    both = mm(jnp.concatenate([coeff_high, coeff_low], 0), high)
    count = coeff_high.shape[0]
    return both[:count] + both[count:] + mm(coeff_high, low)


def put_folded(ref, row, value):
    half, width = value.shape[0] // 2, value.shape[1]
    ref[row : row + half, :width] = value[:half]
    ref[row : row + half, width:] = value[half:]


def get_folded(ref, row, height, width):
    half = height // 2
    return jnp.concatenate([ref[row : row + half, :width], ref[row : row + half, width:]], 0)


def message_rows(levels, rank, rhs, height):
    rows = {"Z": 0}
    at = rank
    if height >= TOP:
        rows["w"] = at
        at += rhs
    if height + 1 < levels:
        rows["p"] = at
        at += rhs
    for upper in range(height + 1, levels - 1):
        rows[upper] = at
        at += rank
    return rows, at


def kernel(levels, scale, tile, *refs):
    x_ref, b_ref, v_ref, t_ref, skel_ref, owner_ref, near_ref, out_ref = refs[:8]
    G, acc, far_acc, norm_row = refs[8:12]
    sent = refs[12 : 12 + levels]
    came = refs[12 + levels : 12 + 2 * levels]
    bulk_send, bulk_recv, tree_send, tree_recv, relay_send, relay_recv = refs[12 + 2 * levels :]
    me = lax.axis_index("leaf")
    points, embed = x_ref.shape
    rhs, rank = b_ref.shape[1], v_ref.shape[1]
    rows_each = points // CHUNKS
    pitch = rows_each + rhs
    tail = CHUNKS * pitch

    def partner(mask):
        where = me
        for bit in range(levels):
            if mask >> bit & 1:
                where = where + (1 << bit) * (1 - 2 * ((me // (1 << bit)) % 2))
        return where

    core = me % 2

    def picks(level, node):
        return as_column(skel_ref[level, pl.ds(node, 1), :])

    def one_hot(column, width, base):
        lane = lax.broadcasted_iota(jnp.int32, (column.shape[0], width), 1) + base
        return jnp.where(lane == column, 1.0, 0.0).astype(BF16)

    near_ids = [near_ref[me, slot] for slot in range(near_ref.shape[1])]

    def near_flag(offset):
        hit = near_ids[0] == offset
        for other in near_ids[1:]:
            hit = hit | (other == offset)
        return jnp.where(hit, 1.0, 0.0)

    b_t = jnp.concatenate([b_ref[...], jnp.zeros_like(b_ref)], 1).T[:rhs]
    b_high, b_low = split(b_t)
    for q in range(CHUNKS):
        G[0, q * pitch : q * pitch + rows_each, :] = x_ref[q * rows_each : (q + 1) * rows_each, :]
        put_folded(G.at[0], q * pitch + rows_each, b_high[:, q * rows_each : (q + 1) * rows_each])
        put_folded(
            G.at[0], q * pitch + rows_each + rhs // 2, b_low[:, q * rows_each : (q + 1) * rows_each]
        )
    w = mm(b_t, v_ref[...], PRECISE)
    w_high, w_low = split(w)
    put_folded(G.at[0], tail, w_high)
    norm_row[...] = as_row(norm_column(x_ref[...], scale))
    pick = picks(0, me)
    Z = mm(one_hot(pick, points, 0), x_ref[...]).astype(BF16)
    leaf_Z = Z
    leaf_Z_row = as_row(norm_column(Z, scale))
    lifts = {}
    for height in range(1, levels - 1):
        mine = me % (1 << height) == owner_ref[height - 1, me // (1 << height)]
        lifts[height] = t_ref[0, height] * jnp.where(mine, 1.0, 0.0)

    layouts = [message_rows(levels, rank, rhs, height) for height in range(levels)]

    def write_message(height, w, Z, partial, lifts):
        rows, _ = layouts[height]
        buf = sent[height]
        buf[0:rank, :] = Z
        for key, value in (("w", w), ("p", partial)):
            if key in rows:
                high, low = split(value)
                put_folded(buf, rows[key], high)
                put_folded(buf, rows[key] + rhs // 2, low)
        for upper in range(height + 1, levels - 1):
            high, low = split(lifts[upper])
            put_folded(buf, rows[upper], high)
            put_folded(buf, rows[upper] + rank // 2, low)

    def read_pair(height, key):
        row = layouts[height][0][key]
        high = get_folded(came[height], row, rhs, rank)
        low = get_folded(came[height], row + rhs // 2, rhs, rank)
        return high, low

    def tree_copy(height):
        size = layouts[height][1]
        if height == 0:
            part = pl.ds(0, size)
        else:
            part = pl.ds(pl.multiple_of(core * (size // 2), 16), size // 2)
        return pltpu.make_async_remote_copy(
            src_ref=sent[height].at[part],
            dst_ref=came[height].at[part],
            send_sem=tree_send.at[height],
            recv_sem=tree_recv.at[height],
            device_id=(partner(1 << height),),
            device_id_type=MESH,
        )

    def relay_copy(height):
        size = layouts[height][1]
        part = pl.ds(pl.multiple_of(core * (size // 2), 16), size // 2)
        return pltpu.make_async_remote_copy(
            src_ref=came[height].at[part],
            dst_ref=came[height].at[part],
            send_sem=relay_send.at[height],
            recv_sem=relay_recv.at[height],
            device_id=(partner(1),),
            device_id_type=MESH,
        )

    def relay_wait(height):
        size = layouts[height][1]
        part = pl.ds(pl.multiple_of((1 - core) * (size // 2), 16), size // 2)
        pltpu.make_async_remote_copy(
            src_ref=came[height].at[part],
            dst_ref=came[height].at[part],
            send_sem=relay_send.at[height],
            recv_sem=relay_recv.at[height],
            device_id=(partner(1),),
            device_id_type=MESH,
        ).wait_recv()

    routes = {1: (0, 1), 2: (0, 2), 4: (0, 4), 3: (2, 1), 5: (4, 1), 7: (6, 1)}

    def bulk(slot, q):
        if slot == 6:
            source, mask = (2, 4) if q < CHUNKS // 2 else (4, 2)
        else:
            source, mask = routes[slot]
        extent = pitch + (rhs // 2 if q == CHUNKS - 1 else 0)
        part = pl.ds(q * pitch, extent)
        return pltpu.make_async_remote_copy(
            src_ref=G.at[source, part],
            dst_ref=G.at[slot, part],
            send_sem=bulk_send.at[slot, q],
            recv_sem=bulk_recv.at[slot, q],
            device_id=(partner(mask),),
            device_id_type=MESH,
        )

    state = {}

    def lift(height, w):
        return mm(w, lifts[height] if height else t_ref[0, 0], PRECISE)

    state["w"], state["Z"], state["C"] = w, Z, {}
    state["partial"] = lift(0, w)
    write_message(0, w, Z, state["partial"], lifts)

    barrier = pltpu.get_barrier_semaphore()
    for bit in range(levels):
        pl.semaphore_signal(barrier, inc=1, device_id=(partner(1 << bit),), device_id_type=MESH)
    pl.semaphore_wait(barrier, levels)

    tree_copy(0).start()
    low_half, high_half = range(CHUNKS // 2), range(CHUNKS // 2, CHUNKS)
    for q, r in zip(low_half, high_half):
        bulk(2, q).start()
        bulk(4, r).start()
    for q in range(CHUNKS):
        bulk(1, q).start()

    acc[...] = jnp.zeros_like(acc)
    far_acc[...] = jnp.zeros_like(far_acc)
    for q in range(CHUNKS):
        own = x_ref[q * rows_each : (q + 1) * rows_each, :]
        own_norm = norm_column(own, scale)
        part = slice(q * rows_each, (q + 1) * rows_each)

        def own_tile(step, carry, own=own, own_norm=own_norm, part=part):
            at = pl.ds(pl.multiple_of(step * tile, tile), tile)
            block = gauss(own, own_norm, x_ref[at, :], norm_row[:, at], scale)
            acc[:, at] += contract_both(b_high[:, part], b_low[:, part], block)
            return carry

        lax.fori_loop(0, points // tile, own_tile, 0)

    def advance(height):
        rows = layouts[height][0]
        sibling_Z = came[height][0:rank, :]
        if height >= TOP:
            high, low = read_pair(height, "w")
            block = gauss(
                sibling_Z,
                norm_column(sibling_Z, scale),
                state["Z"],
                as_row(norm_column(state["Z"], scale)),
                scale,
            )
            state["C"][height] = contract_both(high, low, block)
        if height + 1 == levels:
            return
        high, low = read_pair(height, "p")
        state["w"] = state["partial"] + (high.astype(F32) + low.astype(F32))
        for upper in range(height + 1, levels - 1):
            high = get_folded(came[height], rows[upper], rank, rank)
            low = get_folded(came[height], rows[upper] + rank // 2, rank, rank)
            lifts[upper] = lifts[upper] + (high.astype(F32) + low.astype(F32))
        pick = picks(height + 1, me // (2 << height))
        shift = rank * ((me // (1 << height)) % 2)
        pick = jnp.where(pick >= shift, pick - shift, pick + shift)
        state["Z"] = (
            mm(one_hot(pick, rank, 0), state["Z"]) + mm(one_hot(pick, rank, rank), sibling_Z)
        ).astype(BF16)
        if height + 2 < levels:
            state["partial"] = lift(height + 1, state["w"])
        else:
            state["partial"] = None
        write_message(height + 1, state["w"], state["Z"], state["partial"], lifts)
        tree_copy(height + 1).start()

    tree_copy(0).wait_recv()
    advance(0)
    for q, r in zip(low_half, high_half):
        bulk(2, r).start()
        bulk(4, q).start()

    def arrive(slot, q):
        bulk(slot, q).wait_recv()
        if slot in (2, 4, 6):
            bulk(slot + 1, q).start()
        if (slot == 2 and q < CHUNKS // 2) or (slot == 4 and q >= CHUNKS // 2):
            bulk(6, q).start()

    def near(slot, q):
        at_row = q * pitch
        theirs = G[slot, at_row : at_row + rows_each, :]
        flag = near_flag(slot)
        high = get_folded(G.at[slot], at_row + rows_each, rhs, rows_each)
        low = get_folded(G.at[slot], at_row + rows_each + rhs // 2, rhs, rows_each)
        high = (high.astype(F32) * flag).astype(BF16)
        low = (low.astype(F32) * flag).astype(BF16)
        their_norm = norm_column(theirs, scale)

        def one_tile(step, carry):
            at = pl.ds(pl.multiple_of(step * tile, tile), tile)
            block = gauss(theirs, their_norm, x_ref[at, :], norm_row[:, at], scale)
            acc[:, at] += contract_both(high, low, block)
            return carry

        lax.fori_loop(0, points // tile, one_tile, 0)

    def far(slot):
        pick = picks(0, partner(slot))
        rows = None
        for q in range(CHUNKS):
            term = mm(
                one_hot(pick, rows_each, q * rows_each),
                G[slot, q * pitch : q * pitch + rows_each, :],
            )
            rows = term if rows is None else rows + term
        rows = rows.astype(BF16)
        coeff = get_folded(G.at[slot], tail, rhs, rank)
        coeff = (coeff.astype(F32) * (1.0 - near_flag(slot))).astype(BF16)
        block = gauss(rows, norm_column(rows, scale), leaf_Z, leaf_Z_row, scale)
        far_acc[...] += contract(coeff, block)

    def first_half(height):
        tree_copy(height).wait_recv()
        relay_copy(height).start()

    def second_half(height):
        relay_wait(height)
        advance(height)

    tree_steps = []
    for height in range(1, levels):
        tree_steps.append(functools.partial(first_half, height))
        tree_steps.append(functools.partial(second_half, height))

    def tree_step():
        if tree_steps:
            tree_steps.pop(0)()

    for q in range(CHUNKS):
        arrive(1, q)
        near(1, q)
    far(1)
    orders = [(q, r) for q, r in zip(low_half, high_half)]
    orders += [(r, q) for q, r in zip(low_half, high_half)]
    for q, r in orders:
        arrive(2, q)
        arrive(4, r)
        near(2, q)
        tree_step()
        near(4, r)
        arrive(3, q)
        arrive(5, r)
        near(3, q)
        tree_step()
        near(5, r)
    for slot in (2, 4, 3, 5):
        far(slot)
        tree_step()
    for q, r in zip(low_half, high_half):
        arrive(6, q)
        arrive(6, r)
        near(6, q)
        near(6, r)
    while tree_steps:
        tree_step()

    down = state["C"][levels - 1]
    for height in range(levels - 2, -1, -1):
        down = mm_nt(down, lifts[height] if height else t_ref[0, 0], PRECISE)
        if height in state["C"]:
            down = down + state["C"][height]
    for q in range(CHUNKS):
        arrive(7, q)
        near(7, q)
    far(6)
    far(7)
    total = acc[...] + mm_nt(down + far_acc[...], v_ref[...], PRECISE)
    out_ref[...] = jnp.concatenate([total, jnp.zeros_like(total)], 0).T[:, :rhs]

    for slot in range(1, GROUP):
        for q in range(CHUNKS):
            bulk(slot, q).wait_send()
    for height in range(levels):
        tree_copy(height).wait_send()
        if height:
            relay_copy(height).wait_send()


def solution(mesh):
    leaves = mesh.shape["leaf"]
    levels = leaves.bit_length() - 1

    def per_device(points, weights, leaf_basis, transfer, skeleton_index, node_owner, near_list):
        count, embed = points.shape
        rhs, rank = weights.shape[1], leaf_basis.shape[1]
        pitch = count // CHUNKS + rhs
        vmem = pl.BlockSpec(memory_space=pltpu.VMEM)
        smem = pl.BlockSpec(memory_space=pltpu.SMEM)
        sizes = [message_rows(levels, rank, rhs, height)[1] for height in range(levels)]
        buffers = [pltpu.VMEM((size, embed), BF16) for size in sizes]
        return pl.pallas_call(
            functools.partial(kernel, levels, 2.0 / embed, min(512, count)),
            out_shape=jax.ShapeDtypeStruct((count, rhs), F32),
            in_specs=[vmem] * 5 + [smem] * 2,
            out_specs=vmem,
            scratch_shapes=[
                pltpu.VMEM((GROUP, CHUNKS * pitch + rhs // 2, embed), BF16),
                pltpu.VMEM((rhs, count), F32),
                pltpu.VMEM((rhs, rank), F32),
                pltpu.VMEM((1, count), F32),
                *buffers,
                *buffers,
                pltpu.SemaphoreType.DMA((GROUP, CHUNKS)),
                pltpu.SemaphoreType.DMA((GROUP, CHUNKS)),
                pltpu.SemaphoreType.DMA((levels,)),
                pltpu.SemaphoreType.DMA((levels,)),
                pltpu.SemaphoreType.DMA((levels,)),
                pltpu.SemaphoreType.DMA((levels,)),
            ],
            compiler_params=pltpu.CompilerParams(
                collective_id=0, has_side_effects=True, vmem_limit_bytes=52 * 2**20
            ),
        )(points, weights, leaf_basis, transfer, skeleton_index, node_owner, near_list)

    return jax.shard_map(
        per_device,
        mesh=mesh,
        in_specs=(
            P("leaf", None),
            P("leaf", None),
            P("leaf", None),
            P("leaf", None, None, None),
            P(),
            P(),
            P(),
        ),
        out_specs=P("leaf", None),
        check_vma=False,
    )
```

time: 363 us -> 98.6 us (0.27); the launches traced: 359 us -> 98.5 us
  waiting for transfers between devices: 135 us -> 0 us
  Pallas kernels: 0 us -> 95.6 us
  other arithmetic: 67.3 us -> 0 us
  starting transfers between devices: 57.9 us -> 0 us
  matrix products: 45.8 us -> 0 us
  local copies, waits for them, and re-layouts: 25.6 us -> 2.84 us
  loops' own time: 14.4 us -> 0 us
  between operations: 13.1 us -> 0.03 us
    ppermute x35 -> x0, waiting for transfers between devices: 135 us -> none  [swapped(): return lax.ppermute(value, axis, pairs)]
    pallas_call x0 -> x1, Pallas kernels: none -> 95.6 us  [per_device(): pl.pallas_call(functools.partial(kernel, levels, 2.0 / embed, min(512, co...]
    ppermute x35 -> x0, starting transfers between devices: 57.9 us -> none  [swapped(): return lax.ppermute(value, axis, pairs)]
    dot_general x30 -> x0, matrix products: 45.8 us -> none  [the longest x15 27.1 us: apply_matrix(): jnp.dot(matrix, values, precision=PRECISE, preferred_element_type=jnp.flo...]
    select_n x23 -> x0, other arithmetic: 37.4 us -> none  [the longest x11 28.2 us: join_pair(): jnp.where(upper_half, jnp.concatenate([arrived_part, held_part], 0), jnp....]
    another operation x16 -> x0, loops' own time: 14.4 us -> none  [the longest x8 14 us: per_device(): pushed = lax.cond(wanted, pushed_term, no_term, group_points[target])]
    reduce_sum x12 -> x0, other arithmetic: 12.1 us -> none  [the longest x9 9.77 us: kernel_block(): right_norm = jnp.sum(jnp.square(right_rows.astype(jnp.float32)), axis=1)]
    gather x5 -> x0, local copies, waits for them, and re-layouts: 8.59 us -> none  [the longest x4 5.31 us: per_device(): jnp.take(joined, skeleton_index[height + 1, leaf_index >> height + 1], ax...]
  transfers between devices with their start and end apart: 35 -> 0, of which waited for: 10 -> 0; matrix products, arithmetic and copies ran while one was open for 37% -> 0% of each run, Pallas kernels for 0% -> 0%
where the time goes in v1:
time: 98.6 us; the launch traced here: 98.5 us
  Pallas kernels  95.6 us (97%)
  local copies, waits for them, and re-layouts  2.84 us (3%)
    pallas_call x1, Pallas kernels, per_device(): pl.pallas_call(functools.partial(kernel, levels, 2.0 / embed, min(512, co...  95.6 us

profile of v1, /device:TPU:0, one launch (start us, length us, event | category | flops | bytes accessed | tf_op | source)
XLA Modules:
  0.0 98.5 jit_solution(13993686340741207721)
XLA Ops:
  0.0 0.8 copy.9.refs_6_
  0.8 0.0 copy-start
  0.8 0.0 copy-start.1
  0.8 1.2 %copy.8.refs_1_ = f32[1024,64]{1,0:T(8,128)S(1)} copy(f32[1024,64]{0,1:T(8,128)} %param.8) | data formatting | bytes 524288 | tf_op args[1]
  2.0 0.0 copy-done
  2.0 0.0 copy-done.1
  2.0 95.6 %shard_map.73 = f32[1024,64]{1,0:T(8,128)S(1)} custom-call(bf16[1024,512]{1,0:T(8,128)(2,1)} %refs_0_.1, f32[1024,64]{1,0:T(8,128)S(1)} %copy.8.refs_1_, f32[1024,256]{1,0:T(8,128)} %refs_2_.1, f32[1,4,256,256]{3,2,1,0:T(8,128)} %refs_3_.1, s32[5,32,256]{2,1,0:T(8,128)S(1)} %copy-done, s32[3,32]{1,0:T(4,128)S(1)} %copy-done.1, s32[32,3]{1,0:T(8,128)S(1)} %copy.9.refs_6_), custom_call_target="tpu_custom_call" | custom-call | tf_op jit(solution)/shard_map/pallas_call | solution.py:422
  97.6 0.9 copy.10
Async XLA Ops:
  0.8 1.2 %copy-start = (s32[5,32,256]{2,1,0:T(8,128)S(1)}, s32[5,32,256]{2,1,0:T(8,128)}, u32[]{:S(2)}) copy-start(s32[5,32,256]{2,1,0:T(8,128)} %refs_4_.1) | copy-start | bytes 491524
  0.8 1.2 %copy-start.1 = (s32[3,32]{1,0:T(4,128)S(1)}, s32[3,32]{1,0:T(4,128)}, u32[]{:S(2)}) copy-start(s32[3,32]{1,0:T(4,128)} %refs_5_.1) | copy-start | bytes 1156

commit v2 on v1

--- a/solution.py
+++ b/solution.py
@@ -310,9 +310,11 @@
     def near(slot, q):
         at_row = q * pitch
         theirs = G[slot, at_row : at_row + rows_each, :]
-        flag = near_flag(slot)
-        high = get_folded(G.at[slot], at_row + rows_each, rhs, rows_each)
-        low = get_folded(G.at[slot], at_row + rows_each + rhs // 2, rhs, rows_each)
+        flag = jnp.where(slot > 0, 1.0, 0.0)
+        start, half = at_row + rows_each, rhs // 2
+        both = G[slot, start : start + rhs, :]
+        high = jnp.concatenate([both[:half, :rows_each], both[:half, rows_each:]], 0)
+        low = jnp.concatenate([both[half:, :rows_each], both[half:, rows_each:]], 0)
         high = (high.astype(F32) * flag).astype(BF16)
         low = (low.astype(F32) * flag).astype(BF16)
         their_norm = norm_column(theirs, scale)
@@ -359,29 +361,22 @@
 
     for q in range(CHUNKS):
         arrive(1, q)
-        near(1, q)
     far(1)
     orders = [(q, r) for q, r in zip(low_half, high_half)]
     orders += [(r, q) for q, r in zip(low_half, high_half)]
     for q, r in orders:
         arrive(2, q)
         arrive(4, r)
-        near(2, q)
         tree_step()
-        near(4, r)
         arrive(3, q)
         arrive(5, r)
-        near(3, q)
         tree_step()
-        near(5, r)
     for slot in (2, 4, 3, 5):
         far(slot)
         tree_step()
     for q, r in zip(low_half, high_half):
         arrive(6, q)
         arrive(6, r)
-        near(6, q)
-        near(6, r)
     while tree_steps:
         tree_step()
 
@@ -392,9 +387,11 @@
             down = down + state["C"][height]
     for q in range(CHUNKS):
         arrive(7, q)
-        near(7, q)
     far(6)
     far(7)
+    for slot in near_ids:
+        for q in range(CHUNKS):
+            near(slot, q)
     total = acc[...] + mm_nt(down + far_acc[...], v_ref[...], PRECISE)
     out_ref[...] = jnp.concatenate([total, jnp.zeros_like(total)], 0).T[:, :rhs]
 

time: 98.6 us -> 100 us (1.014)
  Pallas kernels: 95.6 us -> 97.2 us
    pallas_call x1, Pallas kernels: 95.6 us -> 97.2 us  [per_device(): pl.pallas_call(functools.partial(kernel, levels, 2.0 / embed, min(512, co...]
where the time goes in v2:
time: 100 us
  Pallas kernels  97.2 us (97%)
  local copies, waits for them, and re-layouts  2.84 us (3%)
    pallas_call x1, Pallas kernels, per_device(): pl.pallas_call(functools.partial(kernel, levels, 2.0 / embed, min(512, co...  97.2 us

profile of v2, /device:TPU:0, one launch (start us, length us, event | category | flops | bytes accessed | tf_op | source)
XLA Modules:
  0.0 100.0 jit_solution(8377366507615473857)
XLA Ops:
  0.0 0.8 copy.9.refs_6_
  0.8 0.0 copy-start
  0.8 0.0 copy-start.1
  0.8 1.2 %copy.8.refs_1_ = f32[1024,64]{1,0:T(8,128)S(1)} copy(f32[1024,64]{0,1:T(8,128)} %param.8) | data formatting | bytes 524288 | tf_op args[1]
  2.0 0.0 copy-done
  2.0 0.0 copy-done.1
  2.0 97.2 %shard_map.73 = f32[1024,64]{1,0:T(8,128)S(1)} custom-call(bf16[1024,512]{1,0:T(8,128)(2,1)} %refs_0_.1, f32[1024,64]{1,0:T(8,128)S(1)} %copy.8.refs_1_, f32[1024,256]{1,0:T(8,128)} %refs_2_.1, f32[1,4,256,256]{3,2,1,0:T(8,128)} %refs_3_.1, s32[5,32,256]{2,1,0:T(8,128)S(1)} %copy-done, s32[3,32]{1,0:T(4,128)S(1)} %copy-done.1, s32[32,3]{1,0:T(8,128)S(1)} %copy.9.refs_6_), custom_call_target="tpu_custom_call" | custom-call | tf_op jit(solution)/shard_map/pallas_call | solution.py:419
  99.1 0.9 copy.10
Async XLA Ops:
  0.8 1.2 %copy-start = (s32[5,32,256]{2,1,0:T(8,128)S(1)}, s32[5,32,256]{2,1,0:T(8,128)}, u32[]{:S(2)}) copy-start(s32[5,32,256]{2,1,0:T(8,128)} %refs_4_.1) | copy-start | bytes 491524
  0.8 1.2 %copy-start.1 = (s32[3,32]{1,0:T(4,128)S(1)}, s32[3,32]{1,0:T(4,128)}, u32[]{:S(2)}) copy-start(s32[3,32]{1,0:T(4,128)} %refs_5_.1) | copy-start | bytes 1156
